TPU v7x, 32 devices: a whole 2x2x4 slice. The times are simulated.
32 devices in a mesh: lon: 8 (over y, x, core), lat: 4 (over z).
Axes of the slice: x: 2, y: 2, z: 4, core: 2. Of those that a mesh axis runs over, the one named last changes fastest.
Arguments:
- control: float32 [2, 16, 256, 1024], P(None, None, 'lat', 'lon'), may hold values from -6 to 6
- land_mask: int32 [256, 1024], P('lat', 'lon'), may hold values 0 or 1
- std_dev: float32 [2, 16], replicated, may hold values from 0.3 to 3
- innovation: float32 [32, 16, 1024], P(None, 'lat', 'lon'), may hold values from -6 to 6
- inverse_var: float32 [32, 16, 1024], P(None, 'lat', 'lon'), may hold values from 0.25 to 4
- obs_row: int32 [16, 1024], P('lat', 'lon'), may hold values from 0 to 62
- obs_col: int32 [16, 1024], P('lat', 'lon'), may hold values from 0 to 126
- frac_row: float32 [16, 1024], P('lat', 'lon'), may hold values from 0 to 1
- frac_col: float32 [16, 1024], P('lat', 'lon'), may hold values from 0 to 1
- counts: int32 [16, 64], P('lat', 'lon'), may hold values from 0 to 16, as said below
Outputs:
- gradient: float32 [2, 16, 256, 1024], P(None, None, 'lat', 'lon')
Inputs may be any that keep to these rules, and one draw needn't show every extreme that they name: `counts`: each tile gets at most 16 live slots from one holder; in every draw some tile gets exactly 16 from every holder. Dense tiles are drawn from the seed.
All inputs are finite; a program needn't handle non-finite values. No bound on the sum of `land_mask` on one device may be relied on, other than what follows from the above.
Results may differ from a plain program's by a relative error of at most 0.000075.
Values sent between devices are 32-bit elements; how exact they have to be, the bound alone decides.
A program may use at most 64 MiB of HBM per device.

v0:
```python
import jax
import jax.numpy as jnp
from jax import lax
from jax.sharding import PartitionSpec as P

HALF = 50


def padded_2(cells, sides, width):
    for axis, dim in sides:
        count = lax.axis_size(axis)
        head = lax.slice_in_dim(cells, 0, width, axis=dim)
        tail = lax.slice_in_dim(cells, cells.shape[dim] - width, cells.shape[dim], axis=dim)
        cells = jnp.concatenate(
            [
                lax.ppermute(tail, axis, [(i, (i + 1) % count) for i in range(count)]),
                cells,
                lax.ppermute(head, axis, [((i + 1) % count, i) for i in range(count)]),
            ],
            axis=dim,
        )
    return cells


def tap_band(n_out, n_in, offset):
    spread = HALF / 2.0
    whole = jnp.arange(-HALF, HALF + 1).astype(jnp.float32)
    norm = jnp.sqrt(jnp.sum(jnp.exp(-(whole / spread) * (whole / spread))))
    out_index = lax.broadcasted_iota(jnp.int32, (n_out, n_in), 0)
    in_index = lax.broadcasted_iota(jnp.int32, (n_out, n_in), 1)
    reach = in_index - out_index - offset
    inside = (reach >= 0) & (reach <= 2 * HALF)
    distance = (reach - HALF).astype(jnp.float32)
    values = jnp.exp(-0.5 * (distance / spread) * (distance / spread)) / norm
    return jnp.where(inside, values, 0.0)


def along_x(field):
    extended = padded_2(field, (("lon", 2),), HALF)
    width = field.shape[2]
    band = tap_band(width, width + 2 * HALF, 0)
    return jnp.einsum("rye,xe->ryx", extended, band, precision=lax.Precision.HIGHEST)


def filter_whole_lines(lines, block):
    count = lines.shape[1] // block
    padded = jnp.pad(lines, ((0, 0), (block, block), (0, 0)))
    blocks = padded.reshape(lines.shape[0], count + 2, block, lines.shape[2])
    band = tap_band(block, 3 * block, block - HALF)
    output = jnp.einsum(
        "ab,rnbc->rnac", band[:, :block], blocks[:, :-2], precision=lax.Precision.HIGHEST
    )
    output = output + jnp.einsum(
        "ab,rnbc->rnac",
        band[:, block : 2 * block],
        blocks[:, 1:-1],
        precision=lax.Precision.HIGHEST,
    )
    output = output + jnp.einsum(
        "ab,rnbc->rnac", band[:, 2 * block :], blocks[:, 2:], precision=lax.Precision.HIGHEST
    )
    return output.reshape(lines.shape)


def along_y(field):
    height = field.shape[1]
    smoothed = filter_whole_lines(
        lax.all_to_all(field, "lat", split_axis=0, concat_axis=1, tiled=True), height
    )
    return lax.all_to_all(smoothed, "lat", split_axis=1, concat_axis=0, tiled=True)


def shards(
    control,
    land_mask,
    std_dev,
    innovation,
    inverse_var,
    obs_row,
    obs_col,
    frac_row,
    frac_col,
    counts,
):
    rows_total = control.shape[0] * control.shape[1]
    tile_rows = control.shape[2]
    tile_cols = control.shape[3]
    fields = control.reshape(rows_total, tile_rows, tile_cols)
    ocean = land_mask.astype(jnp.float32)
    scales = std_dev.reshape(rows_total, 1, 1)
    increment = scales * ocean * along_y(along_x(ocean * fields))
    table = increment.reshape(rows_total, tile_rows * tile_cols)
    corner = obs_row * tile_cols + obs_col
    stencil = [
        (1.0 - frac_row) * (1.0 - frac_col),
        (1.0 - frac_row) * frac_col,
        frac_row * (1.0 - frac_col),
        frac_row * frac_col,
    ]
    shifts = [0, 1, tile_cols, tile_cols + 1]
    columns = jnp.zeros((rows_total,) + corner.shape, jnp.float32)
    for weight, offset in zip(stencil, shifts):
        columns = columns + weight[None] * jnp.take(table, corner + offset, axis=1)
    at_holder = lax.all_to_all(
        lax.all_to_all(columns, "lon", split_axis=2, concat_axis=2, tiled=True),
        "lat",
        split_axis=1,
        concat_axis=1,
        tiled=True,
    )
    weighted_misfit = inverse_var * (at_holder - innovation)
    at_owner = lax.all_to_all(
        lax.all_to_all(weighted_misfit, "lon", split_axis=2, concat_axis=2, tiled=True),
        "lat",
        split_axis=1,
        concat_axis=1,
        tiled=True,
    )
    slot_width = obs_row.shape[1] // counts.shape[1]
    slot_number = lax.broadcasted_iota(jnp.int32, obs_row.shape, 1) % slot_width
    limits = jnp.repeat(counts, slot_width, axis=1)
    live = (slot_number < limits).astype(jnp.float32)
    misfit = at_owner * live[None]
    index_all = jnp.concatenate([(corner + offset).reshape(-1) for offset in shifts])
    values_all = jnp.concatenate(
        [(weight[None] * misfit).reshape(rows_total, -1) for weight in stencil], axis=1
    )
    spread = (
        jnp.zeros((rows_total, tile_rows * tile_cols), jnp.float32).at[:, index_all].add(values_all)
    )
    weighted = spread.reshape(rows_total, tile_rows, tile_cols) * scales
    gradient = fields + ocean * along_x(along_y(ocean * weighted))
    return gradient.reshape(control.shape)


def solution(mesh):
    in_specs = (
        P(None, None, "lat", "lon"),
        P("lat", "lon"),
        P(),
        P(None, "lat", "lon"),
        P(None, "lat", "lon"),
        P("lat", "lon"),
        P("lat", "lon"),
        P("lat", "lon"),
        P("lat", "lon"),
        P("lat", "lon"),
    )
    out_specs = P(None, None, "lat", "lon")
    return jax.shard_map(shards, mesh=mesh, in_specs=in_specs, out_specs=out_specs, check_vma=False)
```

profile of v0, /device:TPU:1, one launch (start us, length us, event | category | flops | bytes accessed | tf_op | source)
XLA Modules:
  0.0 262.2 jit_solution(7240987722631233245)
XLA Ops:
  9.6 12.9 %collective-permute-done = f32[32,64,50]{1,0,2:T(8,128)S(1)} collective-permute-done((f32[32,64,50]{1,0,2:T(8,128)}, f32[32,64,50]{1,0,2:T(8,128)S(1)}, u32[]{:S(2)}, u32[]{:S(2)}) %collective-permute-start) | collective-permute-done | bytes 409632 | tf_op jit(solution)/shard_map/ppermute | solution.py:16
  23.0 3.6 %collective-permute-done.1 = f32[32,64,50]{1,0,2:T(8,128)} collective-permute-done((f32[32,64,50]{1,0,2:T(8,128)}, f32[32,64,50]{1,0,2:T(8,128)}, u32[]{:S(2)}, u32[]{:S(2)}) %collective-permute-start.1) | collective-permute-done | bytes 409632 | tf_op jit(solution)/shard_map/ppermute | solution.py:18
  31.5 4.6 %all-to-all-start = ((f32[32,64,128]{2,1,0:T(8,128)}), f32[32,64,128]{2,1,0:T(8,128)S(1)}, u32[]{:S(2)}, u32[]{:S(2)}) async-start(f32[32,64,128]{2,1,0:T(8,128)} %fusion), calls=%async_computation | async-start | bytes 2097152 | tf_op jit(solution)/shard_map/all_to_all | solution.py:68
  36.1 25.4 %all-to-all-done = f32[32,64,128]{2,1,0:T(8,128)S(1)} async-done(((f32[32,64,128]{2,1,0:T(8,128)}), f32[32,64,128]{2,1,0:T(8,128)S(1)}, u32[]{:S(2)}, u32[]{:S(2)}) %all-to-all-start) | async-done | bytes 1048608 | tf_op jit(solution)/shard_map/all_to_all | solution.py:68
  66.6 3.5 %all-to-all-start.1 = ((f32[8,256,128]{2,0,1:T(8,128)}), f32[8,256,128]{2,0,1:T(8,128)S(1)}, u32[]{:S(2)}, u32[]{:S(2)}) async-start(f32[8,256,128]{2,0,1:T(8,128)} %copy.201), calls=%async_computation.1 | async-start | bytes 2097152 | tf_op jit(solution)/shard_map/all_to_all | solution.py:70
  70.4 25.4 %all-to-all-done.1 = f32[8,256,128]{2,0,1:T(8,128)S(1)} async-done(((f32[8,256,128]{2,0,1:T(8,128)}), f32[8,256,128]{2,0,1:T(8,128)S(1)}, u32[]{:S(2)}, u32[]{:S(2)}) %all-to-all-start.1) | async-done | bytes 1048608 | tf_op jit(solution)/shard_map/all_to_all | solution.py:70
  98.4 4.1 %multiply_multiply_fusion = f32[32,8192]{0,1:T(8,128)} fusion(f32[32,8192]{0,1:T(8,128)} %copy.204, f32[8192]{0:T(1024)S(1)} %get-tuple-element.16, f32[32]{0:T(128)S(1)} %mul.162), kind=kLoop, calls=%fused_computation.5 | loop fusion | flops 524288 | bytes 2130048 | tf_op jit(solution)/shard_map/mul | solution.py:91
  105.8 3.2 %gather_fusion.1 = f32[512,32]{1,0:T(8,128)S(1)} fusion(f32[32,8192]{0,1:T(8,128)} %multiply_multiply_fusion, s32[1024]{0:T(1024)S(1)} %get-tuple-element.34), kind=kCustom, calls=%fused_computation.1.clone | custom fusion | bytes 133120 | tf_op jit(solution)/shard_map/jit(_take)/gather | solution.py:103
  109.2 3.2 %gather_fusion.2 = f32[512,32]{1,0:T(8,128)S(1)} fusion(f32[32,8192]{0,1:T(8,128)} %multiply_multiply_fusion, s32[1024]{0:T(1024)S(1)} %get-tuple-element.33), kind=kCustom, calls=%fused_computation.2.clone | custom fusion | bytes 133120 | tf_op jit(solution)/shard_map/jit(_take)/gather | solution.py:103
  112.5 3.2 %gather_fusion.3 = f32[512,32]{1,0:T(8,128)S(1)} fusion(f32[32,8192]{0,1:T(8,128)} %multiply_multiply_fusion, s32[1024]{0:T(1024)S(1)} %get-tuple-element.32), kind=kCustom, calls=%fused_computation.3.clone | custom fusion | bytes 133120 | tf_op jit(solution)/shard_map/jit(_take)/gather | solution.py:103
  116.9 4.3 %all-to-all-start.2 = ((f32[8,1,2048]{2,1,0:T(1,128)}), f32[8,1,2048]{2,1,0:T(1,128)S(1)}, u32[]{:S(2)}, u32[]{:S(2)}) async-start(f32[8,1,2048]{2,1,0:T(1,128)} %reshape.349), calls=%async_computation.2 | async-start | bytes 131072 | tf_op jit(solution)/shard_map/all_to_all | solution.py:105
  121.4 4.0 %all-to-all-done.2 = f32[8,1,2048]{2,1,0:T(1,128)S(1)} async-done(((f32[8,1,2048]{2,1,0:T(1,128)}), f32[8,1,2048]{2,1,0:T(1,128)S(1)}, u32[]{:S(2)}, u32[]{:S(2)}) %all-to-all-start.2) | async-done | bytes 65568 | tf_op jit(solution)/shard_map/all_to_all | solution.py:105
  127.7 3.3 %all-to-all-start.3 = ((f32[32,4,128]{2,0,1:T(8,128)}), f32[32,4,128]{2,0,1:T(8,128)S(1)}, u32[]{:S(2)}, u32[]{:S(2)}) async-start(f32[32,4,128]{2,0,1:T(8,128)} %copy.214), calls=%async_computation.3 | async-start | bytes 131072 | tf_op jit(solution)/shard_map/all_to_all | solution.py:104
  131.0 4.5 %all-to-all-done.3 = f32[32,4,128]{2,0,1:T(8,128)S(1)} async-done(((f32[32,4,128]{2,0,1:T(8,128)}), f32[32,4,128]{2,0,1:T(8,128)S(1)}, u32[]{:S(2)}, u32[]{:S(2)}) %all-to-all-start.3) | async-done | bytes 65568 | tf_op jit(solution)/shard_map/all_to_all | solution.py:104
  136.6 5.3 %all-to-all-start.4 = ((f32[8,1,2048]{2,1,0:T(1,128)}), f32[8,1,2048]{2,1,0:T(1,128)S(1)}, u32[]{:S(2)}, u32[]{:S(2)}) async-start(f32[8,1,2048]{2,1,0:T(1,128)} %reshape.351), calls=%async_computation.4 | async-start | bytes 131072 | tf_op jit(solution)/shard_map/all_to_all | solution.py:113
  141.8 4.2 %all-to-all-done.4 = f32[8,1,2048]{2,1,0:T(1,128)S(1)} async-done(((f32[8,1,2048]{2,1,0:T(1,128)}), f32[8,1,2048]{2,1,0:T(1,128)S(1)}, u32[]{:S(2)}, u32[]{:S(2)}) %all-to-all-start.4) | async-done | bytes 65568 | tf_op jit(solution)/shard_map/all_to_all | solution.py:113
  147.7 3.3 %all-to-all-start.5 = ((f32[32,4,128]{2,0,1:T(8,128)}), f32[32,4,128]{2,0,1:T(8,128)S(1)}, u32[]{:S(2)}, u32[]{:S(2)}) async-start(f32[32,4,128]{2,0,1:T(8,128)} %copy.218), calls=%async_computation.5 | async-start | bytes 131072 | tf_op jit(solution)/shard_map/all_to_all | solution.py:112
  151.0 4.5 %all-to-all-done.5 = f32[32,4,128]{2,0,1:T(8,128)S(1)} async-done(((f32[32,4,128]{2,0,1:T(8,128)}), f32[32,4,128]{2,0,1:T(8,128)S(1)}, u32[]{:S(2)}, u32[]{:S(2)}) %all-to-all-start.5) | async-done | bytes 65568 | tf_op jit(solution)/shard_map/all_to_all | solution.py:112
  156.0 13.6 %scatter_custom_fusion = f32[32,8192]{0,1:T(8,128)} fusion(s32[2048]{0:T(1024)S(1)} %bitcast.154, f32[2048,32]{1,0:T(8,128)S(1)} %copy.223, f32[]{:T(128)} %constant.23.clone.1), kind=kCustom, calls=%fused_computation.18 | custom fusion | flops 65536 | bytes 1048580 | tf_op jit(solution)/shard_map/scatter-add | solution.py:129
  172.9 27.2 %all_to_all.92 = f32[32,64,128]{2,1,0:T(8,128)S(1)} all-to-all(f32[32,64,128]{2,1,0:T(8,128)S(1)} %multiply_multiply_fusion.1), channel_id=1, replica_groups=mesh['lon'=8,'lat'=4] {'lat'}, dimensions={0} | all-to-all | bytes 2097152 | tf_op jit(solution)/shard_map/all_to_all | solution.py:68
  204.1 27.2 %all_to_all.93 = f32[8,256,128]{2,0,1:T(8,128)S(1)} all-to-all(f32[8,256,128]{2,0,1:T(8,128)S(1)} %copy.226), channel_id=1, replica_groups=mesh['lon'=8,'lat'=4] {'lat'}, dimensions={1} | all-to-all | bytes 2097152 | tf_op jit(solution)/shard_map/all_to_all | solution.py:70
  237.9 13.4 %collective-permute-done.2 = f32[32,64,50]{1,0,2:T(8,128)S(1)} collective-permute-done((f32[32,64,50]{1,0,2:T(8,128)}, f32[32,64,50]{1,0,2:T(8,128)S(1)}, u32[]{:S(2)}, u32[]{:S(2)}) %collective-permute-start.2) | collective-permute-done | bytes 409632 | tf_op jit(solution)/shard_map/ppermute | solution.py:16
  251.9 4.4 %collective-permute-done.3 = f32[32,64,50]{1,0,2:T(8,128)} collective-permute-done((f32[32,64,50]{1,0,2:T(8,128)}, f32[32,64,50]{1,0,2:T(8,128)}, u32[]{:S(2)}, u32[]{:S(2)}) %collective-permute-start.3) | collective-permute-done | bytes 409632 | tf_op jit(solution)/shard_map/ppermute | solution.py:18
  257.9 4.3 %fusion.17 = f32[32,64,128]{2,1,0:T(8,128)} fusion(f32[32,64,128]{2,1,0:T(8,128)} %bitcast.140, f32[32,64,50]{2,1,0:T(8,128)S(1)} %copy.231, f32[32,64,128]{2,1,0:T(8,128)S(1)} %bitcast.131, f32[32,64,50]{2,1,0:T(8,128)S(1)} %copy.230, f32[64,128]{1,0:T(8,128)S(1)} %get-tuple-element.17, f32[]{:T(128)S(6)} %sqrt.2), kind=kOutput, calls=%fused_computation.25 | convolution fusion | flops 719005184 | bytes 3997700 | tf_op jit(solution)/shard_map/rye,xe->ryx/dot_general | solution.py:42
  (89 shorter events, 48.2 us)
Async XLA Ops:
  4.0 18.4 %collective-permute-start = (f32[32,64,50]{1,0,2:T(8,128)}, f32[32,64,50]{1,0,2:T(8,128)S(1)}, u32[]{:S(2)}, u32[]{:S(2)}) collective-permute-start(f32[32,64,50]{1,0,2:T(8,128)} %copy.196), channel_id=1, source_target_pairs={{0,4},{4,8},{8,12},{12,16},{16,20},{20,24},{24,28},{28,0},{1,5},{5... | collective-permute-start | bytes 1228808 | tf_op jit(solution)/shard_map/ppermute | solution.py:16
  8.2 18.5 %collective-permute-start.1 = (f32[32,64,50]{1,0,2:T(8,128)}, f32[32,64,50]{1,0,2:T(8,128)}, u32[]{:S(2)}, u32[]{:S(2)}) collective-permute-start(f32[32,64,50]{1,0,2:T(8,128)} %copy.197), channel_id=1, source_target_pairs={{4,0},{8,4},{12,8},{16,12},{20,16},{24,20},{28,24},{0,28},{5,1},{9... | collective-permute-start | bytes 1228808 | tf_op jit(solution)/shard_map/ppermute | solution.py:18
  31.5 30.1 %all-to-all-start = ((f32[32,64,128]{2,1,0:T(8,128)}), f32[32,64,128]{2,1,0:T(8,128)S(1)}, u32[]{:S(2)}, u32[]{:S(2)}) async-start(f32[32,64,128]{2,1,0:T(8,128)} %fusion), calls=%async_computation | async-start | bytes 2097152 | tf_op jit(solution)/shard_map/all_to_all | solution.py:68
  65.0 5.2 %copy-start.7 = (f32[2,16]{1,0:T(2,128)S(1)}, f32[2,16]{1,0:T(2,128)}, u32[]{:S(2)}) copy-start(f32[2,16]{1,0:T(2,128)} %param.14) | copy-start | bytes 388
  65.0 5.2 %copy-start.3 = (s32[4,128]{1,0:T(4,128)S(1)}, s32[4,128]{1,0:T(4,128)}, u32[]{:S(2)}) copy-start(s32[4,128]{1,0:T(4,128)} %param.18) | copy-start | bytes 6148
  65.0 5.2 %copy-start.4 = (s32[4,128]{1,0:T(4,128)S(1)}, s32[4,128]{1,0:T(4,128)}, u32[]{:S(2)}) copy-start(s32[4,128]{1,0:T(4,128)} %param.17) | copy-start | bytes 6148
  65.0 5.3 %copy-start.5 = (f32[4,128]{1,0:T(4,128)S(1)}, f32[4,128]{1,0:T(4,128)}, u32[]{:S(2)}) copy-start(f32[4,128]{1,0:T(4,128)} %param.20) | copy-start | bytes 6148
  65.0 5.3 %copy-start.6 = (f32[4,128]{1,0:T(4,128)S(1)}, f32[4,128]{1,0:T(4,128)}, u32[]{:S(2)}) copy-start(f32[4,128]{1,0:T(4,128)} %param.19) | copy-start | bytes 6148
  66.6 29.1 %all-to-all-start.1 = ((f32[8,256,128]{2,0,1:T(8,128)}), f32[8,256,128]{2,0,1:T(8,128)S(1)}, u32[]{:S(2)}, u32[]{:S(2)}) async-start(f32[8,256,128]{2,0,1:T(8,128)} %copy.201), calls=%async_computation.1 | async-start | bytes 2097152 | tf_op jit(solution)/shard_map/all_to_all | solution.py:70
  105.7 15.5 %copy-start.2 = (s32[4,8]{1,0:T(4,128)S(1)}, s32[4,8]{1,0:T(4,128)}, u32[]{:S(2)}) copy-start(s32[4,8]{1,0:T(4,128)} %param.21) | copy-start | bytes 388
  109.1 26.5 %copy-start = (f32[32,4,128]{2,1,0:T(4,128)S(1)}, f32[32,4,128]{2,1,0:T(4,128)}, u32[]{:S(2)}) copy-start(f32[32,4,128]{2,1,0:T(4,128)} %param.16) | copy-start | bytes 196612
  109.1 26.5 %copy-start.1 = (f32[32,4,128]{2,1,0:T(4,128)S(1)}, f32[32,4,128]{2,1,0:T(4,128)}, u32[]{:S(2)}) copy-start(f32[32,4,128]{2,1,0:T(4,128)} %param.15) | copy-start | bytes 196612
  116.9 8.5 %all-to-all-start.2 = ((f32[8,1,2048]{2,1,0:T(1,128)}), f32[8,1,2048]{2,1,0:T(1,128)S(1)}, u32[]{:S(2)}, u32[]{:S(2)}) async-start(f32[8,1,2048]{2,1,0:T(1,128)} %reshape.349), calls=%async_computation.2 | async-start | bytes 131072 | tf_op jit(solution)/shard_map/all_to_all | solution.py:105
  127.7 7.9 %all-to-all-start.3 = ((f32[32,4,128]{2,0,1:T(8,128)}), f32[32,4,128]{2,0,1:T(8,128)S(1)}, u32[]{:S(2)}, u32[]{:S(2)}) async-start(f32[32,4,128]{2,0,1:T(8,128)} %copy.214), calls=%async_computation.3 | async-start | bytes 131072 | tf_op jit(solution)/shard_map/all_to_all | solution.py:104
  136.6 9.5 %all-to-all-start.4 = ((f32[8,1,2048]{2,1,0:T(1,128)}), f32[8,1,2048]{2,1,0:T(1,128)S(1)}, u32[]{:S(2)}, u32[]{:S(2)}) async-start(f32[8,1,2048]{2,1,0:T(1,128)} %reshape.351), calls=%async_computation.4 | async-start | bytes 131072 | tf_op jit(solution)/shard_map/all_to_all | solution.py:113
  147.7 7.9 %all-to-all-start.5 = ((f32[32,4,128]{2,0,1:T(8,128)}), f32[32,4,128]{2,0,1:T(8,128)S(1)}, u32[]{:S(2)}, u32[]{:S(2)}) async-start(f32[32,4,128]{2,0,1:T(8,128)} %copy.218), calls=%async_computation.5 | async-start | bytes 131072 | tf_op jit(solution)/shard_map/all_to_all | solution.py:112
  233.6 17.7 %collective-permute-start.2 = (f32[32,64,50]{1,0,2:T(8,128)}, f32[32,64,50]{1,0,2:T(8,128)S(1)}, u32[]{:S(2)}, u32[]{:S(2)}) collective-permute-start(f32[32,64,50]{1,0,2:T(8,128)} %copy.228), channel_id=1, source_target_pairs={{0,4},{4,8},{8,12},{12,16},{16,20},{20,24},{24,28},{28,0},{1,5},{5... | collective-permute-start | bytes 1228808 | tf_op jit(solution)/shard_map/ppermute | solution.py:16
  237.9 18.3 %collective-permute-start.3 = (f32[32,64,50]{1,0,2:T(8,128)}, f32[32,64,50]{1,0,2:T(8,128)}, u32[]{:S(2)}, u32[]{:S(2)}) collective-permute-start(f32[32,64,50]{1,0,2:T(8,128)} %copy.229), channel_id=1, source_target_pairs={{4,0},{8,4},{12,8},{16,12},{20,16},{24,20},{28,24},{0,28},{5,1},{9... | collective-permute-start | bytes 1228808 | tf_op jit(solution)/shard_map/ppermute | solution.py:18
where the time goes:
time: 263 us; the launch traced here: 262 us
  waiting for transfers between devices  102 us (39%)
  blocking collectives  54.5 us (21%)
  local copies, waits for them, and re-layouts  38.3 us (15%)
  starting transfers between devices  29.7 us (11%)
  other arithmetic  22.4 us (9%)
  matrix products  13.9 us (5%)
    all_to_all x1, blocking collectives, along_y(): lax.all_to_all(smoothed, 'lat', split_axis=1, concat_axis=0, tiled=True)  27.2 us
    all_to_all x1, blocking collectives, along_y(): lax.all_to_all(field, 'lat', split_axis=0, concat_axis=1, tiled=True)  27.2 us
    ppermute x2, waiting for transfers between devices, padded_2(): lax.ppermute(tail, axis, [(i, (i + 1) % count) for i in range(count)])  26.2 us
    all_to_all x1, waiting for transfers between devices, along_y(): lax.all_to_all(field, 'lat', split_axis=0, concat_axis=1, tiled=True)  25.4 us
    all_to_all x1, waiting for transfers between devices, along_y(): lax.all_to_all(smoothed, 'lat', split_axis=1, concat_axis=0, tiled=True)  25.4 us
    scatter-add x1, other arithmetic, shards(): jnp.zeros((rows_total, tile_rows * tile_cols), jnp.float32).at[:, index_all]  13.6 us
    gather x8, local copies, waits for them, and re-layouts, shards(): columns = columns + weight[None] * jnp.take(table, corner + offset, axis=1)  13.3 us
    ppermute x2, waiting for transfers between devices, padded_2(): lax.ppermute(head, axis, [((i + 1) % count, i) for i in range(count)])  8.04 us
  transfers between devices with their start and end apart: 10, of which 10 were waited for; matrix products, arithmetic and copies ran while one was open for 2% of the time, Pallas kernels for 0%

commit v1 on v0

--- a/solution.py
+++ b/solution.py
@@ -4,6 +4,28 @@
 from jax.sharding import PartitionSpec as P
 
 HALF = 50
+
+
+def split_up(x, dim, count):
+    before, after = (x.shape[:dim], x.shape[dim + 1 :])
+    return jnp.moveaxis(x.reshape(*before, count, -1, *after), dim, 0)
+
+
+def in_order(blocks, dim):
+    blocks = jnp.moveaxis(blocks, 0, dim)
+    shape = blocks.shape
+    return blocks.reshape(*shape[:dim], shape[dim] * shape[dim + 1], *shape[dim + 2 :])
+
+
+def exchange_in_pairs(x, axis, split_dim, concat_dim):
+    length, index = (lax.axis_size(axis), lax.axis_index(axis))
+    tiles = split_up(x, split_dim, length)
+    outs = [tiles[index]]
+    for step in range(1, length):
+        sent = tiles[index ^ step]
+        outs.append(lax.ppermute(sent, axis, [(i, i ^ step) for i in range(length)]))
+    tiles = jnp.stack(outs)[index ^ jnp.arange(length)]
+    return in_order(tiles, concat_dim)
 
 
 def padded_2(cells, sides, width):
@@ -64,9 +86,7 @@
 
 def along_y(field):
     height = field.shape[1]
-    smoothed = filter_whole_lines(
-        lax.all_to_all(field, "lat", split_axis=0, concat_axis=1, tiled=True), height
-    )
+    smoothed = filter_whole_lines(exchange_in_pairs(field, "lat", 0, 1), height)
     return lax.all_to_all(smoothed, "lat", split_axis=1, concat_axis=0, tiled=True)
 
 

time: 263 us -> 255 us (0.970)
  blocking collectives: 54.5 us -> 32 us
  starting transfers between devices: 29.7 us -> 37.3 us
  waiting for transfers between devices: 102 us -> 109 us
    ppermute x0 -> x6, waiting for transfers between devices: none -> 32 us  [exchange_in_pairs(): lax.ppermute(sent, axis, [(i, i ^ step) for i in range(length)])]
    all_to_all x1 -> x0, blocking collectives: 27.2 us -> none  [along_y(): lax.all_to_all(field, 'lat', split_axis=0, concat_axis=1, tiled=True)]
    all_to_all x1 -> x0, waiting for transfers between devices: 25.4 us -> none  [along_y(): lax.all_to_all(field, 'lat', split_axis=0, concat_axis=1, tiled=True)]
    ppermute x0 -> x6, starting transfers between devices: none -> 7.29 us  [exchange_in_pairs(): lax.ppermute(sent, axis, [(i, i ^ step) for i in range(length)])]
    all_to_all x1, blocking collectives: 27.2 us -> 32 us  [along_y(): lax.all_to_all(smoothed, 'lat', split_axis=1, concat_axis=0, tiled=True)]
    all_to_all x1 -> x0, starting transfers between devices: 4.59 us -> none  [along_y(): lax.all_to_all(field, 'lat', split_axis=0, concat_axis=1, tiled=True)]
    all_to_all x1, starting transfers between devices: 3.52 us -> 7.72 us  [along_y(): lax.all_to_all(smoothed, 'lat', split_axis=1, concat_axis=0, tiled=True)]
    reshape x1 -> x0, local copies, waits for them, and re-layouts: 3.05 us -> none  [shards(): weighted = spread.reshape(rows_total, tile_rows, tile_cols) * scales]
  transfers between devices with their start and end apart: 10 -> 15, of which waited for: 10 -> 13; matrix products, arithmetic and copies ran while one was open for 2% -> 2% of each run, Pallas kernels for 0% -> 0%
where the time goes in v1:
time: 255 us
  waiting for transfers between devices  109 us (43%)
  local copies, waits for them, and re-layouts  39.5 us (15%)
  starting transfers between devices  37.3 us (15%)
  blocking collectives  32 us (13%)
  other arithmetic  22.7 us (9%)
  matrix products  12.9 us (5%)
    ppermute x6, waiting for transfers between devices, exchange_in_pairs(): lax.ppermute(sent, axis, [(i, i ^ step) for i in range(length)])  32 us
    all_to_all x1, blocking collectives, along_y(): lax.all_to_all(smoothed, 'lat', split_axis=1, concat_axis=0, tiled=True)  32 us
    ppermute x2, waiting for transfers between devices, padded_2(): lax.ppermute(tail, axis, [(i, (i + 1) % count) for i in range(count)])  26 us
    all_to_all x1, waiting for transfers between devices, along_y(): lax.all_to_all(smoothed, 'lat', split_axis=1, concat_axis=0, tiled=True)  25.2 us
    scatter-add x1, other arithmetic, shards(): jnp.zeros((rows_total, tile_rows * tile_cols), jnp.float32).at[:, index_all]  13.6 us
    gather x8, local copies, waits for them, and re-layouts, shards(): columns = columns + weight[None] * jnp.take(table, corner + offset, axis=1)  13.3 us
    ppermute x2, waiting for transfers between devices, padded_2(): lax.ppermute(head, axis, [((i + 1) % count, i) for i in range(count)])  8.44 us
    all_to_all x1, starting transfers between devices, along_y(): lax.all_to_all(smoothed, 'lat', split_axis=1, concat_axis=0, tiled=True)  7.72 us
  transfers between devices with their start and end apart: 15, of which 13 were waited for; matrix products, arithmetic and copies ran while one was open for 2% of the time, Pallas kernels for 0%

profile of v1, /device:TPU:1, one launch (start us, length us, event | category | flops | bytes accessed | tf_op | source)
XLA Modules:
  0.0 254.5 jit_solution(14719730365588943019)
XLA Ops:
  9.5 12.9 %collective-permute-done = f32[32,64,50]{1,0,2:T(8,128)S(1)} collective-permute-done((f32[32,64,50]{1,0,2:T(8,128)}, f32[32,64,50]{1,0,2:T(8,128)S(1)}, u32[]{:S(2)}, u32[]{:S(2)}) %collective-permute-start) | collective-permute-done | bytes 409632 | tf_op jit(solution)/shard_map/ppermute | solution.py:38
  23.0 3.6 %collective-permute-done.1 = f32[32,64,50]{1,0,2:T(8,128)} collective-permute-done((f32[32,64,50]{1,0,2:T(8,128)}, f32[32,64,50]{1,0,2:T(8,128)}, u32[]{:S(2)}, u32[]{:S(2)}) %collective-permute-start.1) | collective-permute-done | bytes 409632 | tf_op jit(solution)/shard_map/ppermute | solution.py:40
  34.3 8.8 %collective-permute-done.2 = f32[8,64,128]{2,1,0:T(8,128)S(1)} collective-permute-done((f32[8,64,128]{2,1,0:T(8,128)S(1)}, f32[8,64,128]{2,1,0:T(8,128)S(1)}, u32[]{:S(2)}, u32[]{:S(2)}) %collective-permute-start.2) | collective-permute-done | bytes 262176 | tf_op jit(solution)/shard_map/ppermute | solution.py:26
  43.1 9.0 %collective-permute-done.3 = f32[8,64,128]{2,1,0:T(8,128)S(1)} collective-permute-done((f32[8,64,128]{2,1,0:T(8,128)S(1)}, f32[8,64,128]{2,1,0:T(8,128)S(1)}, u32[]{:S(2)}, u32[]{:S(2)}) %collective-permute-start.3) | collective-permute-done | bytes 262176 | tf_op jit(solution)/shard_map/ppermute | solution.py:26
  57.9 7.7 %all-to-all-start = ((f32[8,256,128]{2,0,1:T(8,128)}), f32[8,256,128]{2,0,1:T(8,128)S(1)}, u32[]{:S(2)}, u32[]{:S(2)}) async-start(f32[8,256,128]{2,0,1:T(8,128)} %copy.199), calls=%async_computation | async-start | bytes 2097152 | tf_op jit(solution)/shard_map/all_to_all | solution.py:90
  65.8 25.2 %all-to-all-done = f32[8,256,128]{2,0,1:T(8,128)S(1)} async-done(((f32[8,256,128]{2,0,1:T(8,128)}), f32[8,256,128]{2,0,1:T(8,128)S(1)}, u32[]{:S(2)}, u32[]{:S(2)}) %all-to-all-start) | async-done | bytes 1048608 | tf_op jit(solution)/shard_map/all_to_all | solution.py:90
  93.7 4.2 %multiply_multiply_fusion = f32[32,8192]{0,1:T(8,128)} fusion(f32[32,8192]{0,1:T(8,128)} %copy.202, f32[8192]{0:T(1024)S(1)} %get-tuple-element.24, f32[32]{0:T(128)S(1)} %mul.169), kind=kLoop, calls=%fused_computation.7 | loop fusion | flops 524288 | bytes 2130048 | tf_op jit(solution)/shard_map/mul | solution.py:111
  101.2 3.2 %gather_fusion.3 = f32[512,32]{1,0:T(8,128)S(1)} fusion(f32[32,8192]{0,1:T(8,128)} %multiply_multiply_fusion, s32[1024]{0:T(1024)S(1)} %get-tuple-element.42), kind=kCustom, calls=%fused_computation.1.clone | custom fusion | bytes 133120 | tf_op jit(solution)/shard_map/jit(_take)/gather | solution.py:123
  112.3 4.6 %all-to-all-start.1 = ((f32[8,1,2048]{2,1,0:T(1,128)}), f32[8,1,2048]{2,1,0:T(1,128)S(1)}, u32[]{:S(2)}, u32[]{:S(2)}) async-start(f32[8,1,2048]{2,1,0:T(1,128)} %reshape.397), calls=%async_computation.1 | async-start | bytes 131072 | tf_op jit(solution)/shard_map/all_to_all | solution.py:125
  117.0 4.0 %all-to-all-done.1 = f32[8,1,2048]{2,1,0:T(1,128)S(1)} async-done(((f32[8,1,2048]{2,1,0:T(1,128)}), f32[8,1,2048]{2,1,0:T(1,128)S(1)}, u32[]{:S(2)}, u32[]{:S(2)}) %all-to-all-start.1) | async-done | bytes 65568 | tf_op jit(solution)/shard_map/all_to_all | solution.py:125
  123.3 3.3 %all-to-all-start.2 = ((f32[32,4,128]{2,0,1:T(8,128)}), f32[32,4,128]{2,0,1:T(8,128)S(1)}, u32[]{:S(2)}, u32[]{:S(2)}) async-start(f32[32,4,128]{2,0,1:T(8,128)} %copy.212), calls=%async_computation.2 | async-start | bytes 131072 | tf_op jit(solution)/shard_map/all_to_all | solution.py:124
  126.6 4.5 %all-to-all-done.2 = f32[32,4,128]{2,0,1:T(8,128)S(1)} async-done(((f32[32,4,128]{2,0,1:T(8,128)}), f32[32,4,128]{2,0,1:T(8,128)S(1)}, u32[]{:S(2)}, u32[]{:S(2)}) %all-to-all-start.2) | async-done | bytes 65568 | tf_op jit(solution)/shard_map/all_to_all | solution.py:124
  132.2 5.3 %all-to-all-start.3 = ((f32[8,1,2048]{2,1,0:T(1,128)}), f32[8,1,2048]{2,1,0:T(1,128)S(1)}, u32[]{:S(2)}, u32[]{:S(2)}) async-start(f32[8,1,2048]{2,1,0:T(1,128)} %reshape.399), calls=%async_computation.3 | async-start | bytes 131072 | tf_op jit(solution)/shard_map/all_to_all | solution.py:133
  137.4 4.2 %all-to-all-done.3 = f32[8,1,2048]{2,1,0:T(1,128)S(1)} async-done(((f32[8,1,2048]{2,1,0:T(1,128)}), f32[8,1,2048]{2,1,0:T(1,128)S(1)}, u32[]{:S(2)}, u32[]{:S(2)}) %all-to-all-start.3) | async-done | bytes 65568 | tf_op jit(solution)/shard_map/all_to_all | solution.py:133
  143.3 3.3 %all-to-all-start.4 = ((f32[32,4,128]{2,0,1:T(8,128)}), f32[32,4,128]{2,0,1:T(8,128)S(1)}, u32[]{:S(2)}, u32[]{:S(2)}) async-start(f32[32,4,128]{2,0,1:T(8,128)} %copy.216), calls=%async_computation.4 | async-start | bytes 131072 | tf_op jit(solution)/shard_map/all_to_all | solution.py:132
  146.7 4.5 %all-to-all-done.4 = f32[32,4,128]{2,0,1:T(8,128)S(1)} async-done(((f32[32,4,128]{2,0,1:T(8,128)}), f32[32,4,128]{2,0,1:T(8,128)S(1)}, u32[]{:S(2)}, u32[]{:S(2)}) %all-to-all-start.4) | async-done | bytes 65568 | tf_op jit(solution)/shard_map/all_to_all | solution.py:132
  151.6 13.6 %scatter_custom_fusion = f32[32,8192]{0,1:T(8,128)} fusion(s32[2048]{0:T(1024)S(1)} %bitcast.183, f32[2048,32]{1,0:T(8,128)S(1)} %copy.221, f32[]{:T(128)} %constant.27.clone.1), kind=kCustom, calls=%fused_computation.20 | custom fusion | flops 65536 | bytes 1048580 | tf_op jit(solution)/shard_map/scatter-add | solution.py:149
  172.1 6.6 %collective-permute-done.5 = f32[8,64,128]{2,1,0:T(8,128)S(1)} collective-permute-done((f32[8,64,128]{2,1,0:T(8,128)S(1)}, f32[8,64,128]{2,1,0:T(8,128)S(1)}, u32[]{:S(2)}, u32[]{:S(2)}) %collective-permute-start.5) | collective-permute-done | bytes 262176 | tf_op jit(solution)/shard_map/ppermute | solution.py:26
  178.8 7.6 %collective-permute-done.7 = f32[8,64,128]{2,1,0:T(8,128)S(1)} collective-permute-done((f32[8,64,128]{2,1,0:T(8,128)S(1)}, f32[8,64,128]{2,1,0:T(8,128)S(1)}, u32[]{:S(2)}, u32[]{:S(2)}) %collective-permute-start.7) | collective-permute-done | bytes 262176 | tf_op jit(solution)/shard_map/ppermute | solution.py:26
  191.2 32.0 %all_to_all.56 = f32[8,256,128]{2,0,1:T(8,128)S(1)} all-to-all(f32[8,256,128]{2,0,1:T(8,128)S(1)} %copy.224), channel_id=1, replica_groups=mesh['lon'=8,'lat'=4] {'lat'}, dimensions={1} | all-to-all | bytes 2097152 | tf_op jit(solution)/shard_map/all_to_all | solution.py:90
  225.3 3.3 %collective-permute-start.8 = (f32[32,64,50]{1,0,2:T(8,128)}, f32[32,64,50]{1,0,2:T(8,128)S(1)}, u32[]{:S(2)}, u32[]{:S(2)}) collective-permute-start(f32[32,64,50]{1,0,2:T(8,128)} %copy.226), channel_id=1, source_target_pairs={{0,4},{4,8},{8,12},{12,16},{16,20},{20,24},{24,28},{28,0},{1,5},{5... | collective-permute-start | bytes 1228808 | tf_op jit(solution)/shard_map/ppermute | solution.py:38
  230.1 13.0 %collective-permute-done.8 = f32[32,64,50]{1,0,2:T(8,128)S(1)} collective-permute-done((f32[32,64,50]{1,0,2:T(8,128)}, f32[32,64,50]{1,0,2:T(8,128)S(1)}, u32[]{:S(2)}, u32[]{:S(2)}) %collective-permute-start.8) | collective-permute-done | bytes 409632 | tf_op jit(solution)/shard_map/ppermute | solution.py:38
  243.7 4.8 %collective-permute-done.9 = f32[32,64,50]{1,0,2:T(8,128)} collective-permute-done((f32[32,64,50]{1,0,2:T(8,128)}, f32[32,64,50]{1,0,2:T(8,128)}, u32[]{:S(2)}, u32[]{:S(2)}) %collective-permute-start.9) | collective-permute-done | bytes 409632 | tf_op jit(solution)/shard_map/ppermute | solution.py:40
  250.2 4.3 %fusion.17 = f32[32,64,128]{2,1,0:T(8,128)} fusion(f32[32,64,128]{2,1,0:T(8,128)} %bitcast.163, f32[32,64,50]{2,1,0:T(8,128)S(1)} %copy.229, f32[32,64,128]{2,1,0:T(8,128)S(1)} %bitcast.152, f32[32,64,50]{2,1,0:T(8,128)S(1)} %copy.228, f32[64,128]{1,0:T(8,128)S(1)} %get-tuple-element.25, f32[]{:T(128)S(6)} %sqrt.2), kind=kOutput, calls=%fused_computation.27 | convolution fusion | flops 719005184 | bytes 3997700 | tf_op jit(solution)/shard_map/rye,xe->ryx/dot_general | solution.py:64
  (107 shorter events, 59.7 us)
Async XLA Ops:
  4.0 18.4 %collective-permute-start = (f32[32,64,50]{1,0,2:T(8,128)}, f32[32,64,50]{1,0,2:T(8,128)S(1)}, u32[]{:S(2)}, u32[]{:S(2)}) collective-permute-start(f32[32,64,50]{1,0,2:T(8,128)} %copy.194), channel_id=1, source_target_pairs={{0,4},{4,8},{8,12},{12,16},{16,20},{20,24},{24,28},{28,0},{1,5},{5... | collective-permute-start | bytes 1228808 | tf_op jit(solution)/shard_map/ppermute | solution.py:38
  8.2 18.5 %collective-permute-start.1 = (f32[32,64,50]{1,0,2:T(8,128)}, f32[32,64,50]{1,0,2:T(8,128)}, u32[]{:S(2)}, u32[]{:S(2)}) collective-permute-start(f32[32,64,50]{1,0,2:T(8,128)} %copy.195), channel_id=1, source_target_pairs={{4,0},{8,4},{12,8},{16,12},{20,16},{24,20},{28,24},{0,28},{5,1},{9... | collective-permute-start | bytes 1228808 | tf_op jit(solution)/shard_map/ppermute | solution.py:40
  30.6 12.5 %collective-permute-start.2 = (f32[8,64,128]{2,1,0:T(8,128)S(1)}, f32[8,64,128]{2,1,0:T(8,128)S(1)}, u32[]{:S(2)}, u32[]{:S(2)}) collective-permute-start(f32[8,64,128]{2,1,0:T(8,128)S(1)} %get-tuple-element.17), channel_id=1, source_target_pairs={{0,1},{1,0},{2,3},{3,2},{4,5},{5,4},{6,7},{7,6},{8,9},{9,8},{10,11... | collective-permute-start | bytes 786440 | tf_op jit(solution)/shard_map/ppermute | solution.py:26
  32.0 20.1 %collective-permute-start.3 = (f32[8,64,128]{2,1,0:T(8,128)S(1)}, f32[8,64,128]{2,1,0:T(8,128)S(1)}, u32[]{:S(2)}, u32[]{:S(2)}) collective-permute-start(f32[8,64,128]{2,1,0:T(8,128)S(1)} %get-tuple-element.16), channel_id=1, source_target_pairs={{0,2},{1,3},{2,0},{3,1},{4,6},{5,7},{6,4},{7,5},{8,10},{9,11},{10,... | collective-permute-start | bytes 786440 | tf_op jit(solution)/shard_map/ppermute | solution.py:26
  34.3 17.8 %collective-permute-start.4 = (f32[8,64,128]{2,1,0:T(8,128)S(1)}, f32[8,64,128]{2,1,0:T(8,128)S(1)}, u32[]{:S(2)}, u32[]{:S(2)}) collective-permute-start(f32[8,64,128]{2,1,0:T(8,128)S(1)} %get-tuple-element.15), channel_id=1, source_target_pairs={{0,3},{1,2},{2,1},{3,0},{4,7},{5,6},{6,5},{7,4},{8,11},{9,10},{10,... | collective-permute-start | bytes 786440 | tf_op jit(solution)/shard_map/ppermute | solution.py:26
  56.3 9.4 %copy-start.7 = (f32[2,16]{1,0:T(2,128)S(1)}, f32[2,16]{1,0:T(2,128)}, u32[]{:S(2)}) copy-start(f32[2,16]{1,0:T(2,128)} %param.14) | copy-start | bytes 388
  56.3 9.4 %copy-start.3 = (s32[4,128]{1,0:T(4,128)S(1)}, s32[4,128]{1,0:T(4,128)}, u32[]{:S(2)}) copy-start(s32[4,128]{1,0:T(4,128)} %param.18) | copy-start | bytes 6148
  56.3 9.4 %copy-start.4 = (s32[4,128]{1,0:T(4,128)S(1)}, s32[4,128]{1,0:T(4,128)}, u32[]{:S(2)}) copy-start(s32[4,128]{1,0:T(4,128)} %param.17) | copy-start | bytes 6148
  56.3 9.5 %copy-start.5 = (f32[4,128]{1,0:T(4,128)S(1)}, f32[4,128]{1,0:T(4,128)}, u32[]{:S(2)}) copy-start(f32[4,128]{1,0:T(4,128)} %param.20) | copy-start | bytes 6148
  56.3 9.5 %copy-start.6 = (f32[4,128]{1,0:T(4,128)S(1)}, f32[4,128]{1,0:T(4,128)}, u32[]{:S(2)}) copy-start(f32[4,128]{1,0:T(4,128)} %param.19) | copy-start | bytes 6148
  57.9 33.1 %all-to-all-start = ((f32[8,256,128]{2,0,1:T(8,128)}), f32[8,256,128]{2,0,1:T(8,128)S(1)}, u32[]{:S(2)}, u32[]{:S(2)}) async-start(f32[8,256,128]{2,0,1:T(8,128)} %copy.199), calls=%async_computation | async-start | bytes 2097152 | tf_op jit(solution)/shard_map/all_to_all | solution.py:90
  101.1 15.8 %copy-start.2 = (s32[4,8]{1,0:T(4,128)S(1)}, s32[4,8]{1,0:T(4,128)}, u32[]{:S(2)}) copy-start(s32[4,8]{1,0:T(4,128)} %param.21) | copy-start | bytes 388
  104.4 26.7 %copy-start = (f32[32,4,128]{2,1,0:T(4,128)S(1)}, f32[32,4,128]{2,1,0:T(4,128)}, u32[]{:S(2)}) copy-start(f32[32,4,128]{2,1,0:T(4,128)} %param.16) | copy-start | bytes 196612
  104.5 26.7 %copy-start.1 = (f32[32,4,128]{2,1,0:T(4,128)S(1)}, f32[32,4,128]{2,1,0:T(4,128)}, u32[]{:S(2)}) copy-start(f32[32,4,128]{2,1,0:T(4,128)} %param.15) | copy-start | bytes 196612
  112.3 8.8 %all-to-all-start.1 = ((f32[8,1,2048]{2,1,0:T(1,128)}), f32[8,1,2048]{2,1,0:T(1,128)S(1)}, u32[]{:S(2)}, u32[]{:S(2)}) async-start(f32[8,1,2048]{2,1,0:T(1,128)} %reshape.397), calls=%async_computation.1 | async-start | bytes 131072 | tf_op jit(solution)/shard_map/all_to_all | solution.py:125
  123.3 7.9 %all-to-all-start.2 = ((f32[32,4,128]{2,0,1:T(8,128)}), f32[32,4,128]{2,0,1:T(8,128)S(1)}, u32[]{:S(2)}, u32[]{:S(2)}) async-start(f32[32,4,128]{2,0,1:T(8,128)} %copy.212), calls=%async_computation.2 | async-start | bytes 131072 | tf_op jit(solution)/shard_map/all_to_all | solution.py:124
  132.2 9.5 %all-to-all-start.3 = ((f32[8,1,2048]{2,1,0:T(1,128)}), f32[8,1,2048]{2,1,0:T(1,128)S(1)}, u32[]{:S(2)}, u32[]{:S(2)}) async-start(f32[8,1,2048]{2,1,0:T(1,128)} %reshape.399), calls=%async_computation.3 | async-start | bytes 131072 | tf_op jit(solution)/shard_map/all_to_all | solution.py:133
  143.3 7.9 %all-to-all-start.4 = ((f32[32,4,128]{2,0,1:T(8,128)}), f32[32,4,128]{2,0,1:T(8,128)S(1)}, u32[]{:S(2)}, u32[]{:S(2)}) async-start(f32[32,4,128]{2,0,1:T(8,128)} %copy.216), calls=%async_computation.4 | async-start | bytes 131072 | tf_op jit(solution)/shard_map/all_to_all | solution.py:132
  168.5 10.3 %collective-permute-start.5 = (f32[8,64,128]{2,1,0:T(8,128)S(1)}, f32[8,64,128]{2,1,0:T(8,128)S(1)}, u32[]{:S(2)}, u32[]{:S(2)}) collective-permute-start(f32[8,64,128]{2,1,0:T(8,128)S(1)} %get-tuple-element.13), channel_id=1, source_target_pairs={{0,1},{1,0},{2,3},{3,2},{4,5},{5,4},{6,7},{7,6},{8,9},{9,8},{10,11... | collective-permute-start | bytes 786440 | tf_op jit(solution)/shard_map/ppermute | solution.py:26
  169.2 9.6 %collective-permute-start.6 = (f32[8,64,128]{2,1,0:T(8,128)S(1)}, f32[8,64,128]{2,1,0:T(8,128)S(1)}, u32[]{:S(2)}, u32[]{:S(2)}) collective-permute-start(f32[8,64,128]{2,1,0:T(8,128)S(1)} %get-tuple-element.12), channel_id=1, source_target_pairs={{0,2},{1,3},{2,0},{3,1},{4,6},{5,7},{6,4},{7,5},{8,10},{9,11},{10,... | collective-permute-start | bytes 786440 | tf_op jit(solution)/shard_map/ppermute | solution.py:26
  169.5 16.8 %collective-permute-start.7 = (f32[8,64,128]{2,1,0:T(8,128)S(1)}, f32[8,64,128]{2,1,0:T(8,128)S(1)}, u32[]{:S(2)}, u32[]{:S(2)}) collective-permute-start(f32[8,64,128]{2,1,0:T(8,128)S(1)} %get-tuple-element.11), channel_id=1, source_target_pairs={{0,3},{1,2},{2,1},{3,0},{4,7},{5,6},{6,5},{7,4},{8,11},{9,10},{10,... | collective-permute-start | bytes 786440 | tf_op jit(solution)/shard_map/ppermute | solution.py:26
  225.3 17.8 %collective-permute-start.8 = (f32[32,64,50]{1,0,2:T(8,128)}, f32[32,64,50]{1,0,2:T(8,128)S(1)}, u32[]{:S(2)}, u32[]{:S(2)}) collective-permute-start(f32[32,64,50]{1,0,2:T(8,128)} %copy.226), channel_id=1, source_target_pairs={{0,4},{4,8},{8,12},{12,16},{16,20},{20,24},{24,28},{28,0},{1,5},{5... | collective-permute-start | bytes 1228808 | tf_op jit(solution)/shard_map/ppermute | solution.py:38
  230.1 18.4 %collective-permute-start.9 = (f32[32,64,50]{1,0,2:T(8,128)}, f32[32,64,50]{1,0,2:T(8,128)}, u32[]{:S(2)}, u32[]{:S(2)}) collective-permute-start(f32[32,64,50]{1,0,2:T(8,128)} %copy.227), channel_id=1, source_target_pairs={{4,0},{8,4},{12,8},{16,12},{20,16},{24,20},{28,24},{0,28},{5,1},{9... | collective-permute-start | bytes 1228808 | tf_op jit(solution)/shard_map/ppermute | solution.py:40
